TPU v7x, 128 devices: a whole 4x4x4 slice. The times are simulated.
128 devices in a mesh: prow: 8 (over z, core), pcol: 16 (over y, x).
Axes of the slice: x: 4, y: 4, z: 4, core: 2. Of those that a mesh axis runs over, the one named last changes fastest.
Arguments:
- grad_trailing: float32 [8, 8, 256, 4, 16, 256], P(None, 'prow', None, None, 'pcol'), may hold values from -1 to 1, as said below
- panel_one: float32 [8, 8, 256, 256], P(None, 'prow'), may hold values from -6 to 6
- panel_two: float32 [8, 8, 256, 256], P(None, 'prow'), may hold values from -6 to 6
- grad_one: float32 [8, 8, 256, 256], P(None, 'prow'), may hold values from -6 to 6
- grad_two: float32 [8, 8, 256, 256], P(None, 'prow'), may hold values from -6 to 6
- inv_one: float32 [256, 256], replicated, may hold values from -2 to 2, as said below
- inv_two: float32 [256, 256], replicated, may hold values from -2 to 2, as said below
Outputs:
- grad_cols_one: float32 [8, 8, 256, 256], P(None, 'prow')
- grad_cols_two: float32 [8, 8, 256, 256], P(None, 'prow')
- grad_diag_one: float32 [256, 256], replicated
- grad_diag_two: float32 [256, 256], replicated
Inputs may be any that keep to these rules, and one draw needn't show every extreme that they name: `grad_trailing`: G is symmetric: the entry at matrix position (a, b) equals the one at (b, a). `inv_one`: lower triangular; the diagonal lies between 0.8 and 1.6. `inv_two`: lower triangular; the diagonal lies between 0.8 and 1.6.
All inputs are finite; a program needn't handle non-finite values.
Results may differ from a plain program's by a relative error of at most 0.000076.
Values sent between devices are 32-bit elements; how exact they have to be, the bound alone decides.
A program may use at most 128 MiB of HBM per device.

v0:
```python
import math

import jax
import jax.numpy as jnp
from jax import lax
from jax.experimental import pallas as pl
from jax.experimental.pallas import tpu as pltpu
from jax.sharding import PartitionSpec as P

N = 16384
B = 256
HALF = B // 2
QUARTER = B // 4
SCALE = 1.0 / math.sqrt(N)
F32 = jnp.float32
BF16 = jnp.bfloat16

CHILDREN = (1, 0, 0, 0, 11, 7, 5, 4, 9, 1, 1, 1, 0, 0, 0, 0)
DEPTH = (0, 3, 4, 3, 1, 2, 3, 2, 2, 3, 4, 3, 3, 4, 5, 4)
DEEPEST = max(DEPTH)
BLOCKS = 8
STEPS = BLOCKS + 4 + DEEPEST


def split(value):
    high = value.astype(BF16)
    return high, (value - high.astype(F32)).astype(BF16)


def mm(left, right):
    return jnp.dot(left, right, preferred_element_type=F32)


def dot3(left, right):
    lh, ll = split(left)
    rh, rl = split(right)
    return mm(lh, rh) + (mm(lh, rl) + mm(ll, rh))


def lookup(table, index):
    found = jnp.int32(table[0])
    for at in range(1, len(table)):
        found = jnp.where(index == at, jnp.int32(table[at]), found)
    return found


def kernel(
    g_hbm, l1_hbm, l2_hbm, h1_hbm, h2_hbm, w1_ref, w2_ref,
    a1_hbm, a2_hbm, d1_hbm, d2_hbm,
    gbuf, ghi, glo, lbuf, lthi, ltlo, hbuf, kbuf, zbuf, pbuf, xbuf, cbuf, sbuf, obuf,
    dacc2, dacc1, rs2, rs1, dfull, xfull,
    gsem, lsem, hsem, ksend, krecv, xsend, xrecv, csend, crecv, tsend, trecv, osem,
    rsend, rrecv, bsend, drecv, vsend, xxsend, xxrecv,
):
    p = lax.axis_index("prow")
    q = lax.axis_index("pcol")
    z, c = p // 2, p % 2
    y, x = q // 4, q % 4
    zd, cd = (q % 8) // 2, q % 2
    k = (z - zd + 4) % 4
    off_chip = k != 0
    is_dest = q % 8 == p
    helper = jnp.logical_and(k == 0, c != cd)
    pos = jnp.where(c == 0, k - 1, 3 - k)
    home = 2 * zd + cd
    is_root = jnp.logical_and(p == 0, q == 0)

    def remote(src, dst, send, recv, pp, qq):
        return pltpu.make_async_remote_copy(
            src_ref=src, dst_ref=dst, send_sem=send, recv_sem=recv,
            device_id={"prow": pp, "pcol": qq}, device_id_type=pl.DeviceIdType.MESH,
        )

    def load_l(panel):
        src = (l2_hbm, l1_hbm)[panel]
        return pltpu.make_async_copy(src.at[:, 0], lbuf.at[panel], lsem.at[panel])

    def load_g(col):
        return pltpu.make_async_copy(g_hbm.at[:, 0, :, col, 0, :], gbuf.at[col], gsem.at[col])

    def load_h(panel, col):
        src = (h2_hbm, h1_hbm)[panel]
        return pltpu.make_async_copy(src.at[2 * col + q // 8, 0], hbuf.at[panel, col], hsem.at[panel, col])

    load_l(0).start()
    load_l(1).start()
    for i in range(4):
        load_g((i + 1) % 4).start()

    @pl.when(is_dest)
    def _():
        for panel in range(2):
            for i in range(4):
                load_h(panel, (i + 1) % 4).start()

    barrier = pltpu.get_barrier_semaphore()

    def greet(pp, qq):
        pl.semaphore_signal(
            barrier, inc=1, device_id={"prow": pp, "pcol": qq}, device_id_type=pl.DeviceIdType.MESH
        )

    def greet_column(i, _):
        greet((p + i) % 8, q)
        return 0

    def greet_plane(i, _):
        greet(p, (q + i) % 16)
        return 0

    def greet_dest(i, _):
        other = (q + i) % 16

        @pl.when(i != 8)
        def _():
            greet(other % 8, other)

        return 0

    lax.fori_loop(1, 8, greet_column, 0)
    lax.fori_loop(1, 16, greet_plane, 0)

    @pl.when(is_dest)
    def _():
        lax.fori_loop(1, 16, greet_dest, 0)

    for panel in range(2):
        load_l(panel).wait()

        def turn(kb, _, panel=panel):
            hi, lo = split(lbuf[panel, kb].T)
            at = pl.ds(pl.multiple_of(kb * B, B), B)
            lthi[panel * B:(panel + 1) * B, at] = hi
            ltlo[panel * B:(panel + 1) * B, at] = lo
            return 0

        lax.fori_loop(0, 8, turn, 0)

    @pl.when(is_dest)
    def _():
        pl.semaphore_wait(barrier, 36)

    @pl.when(jnp.logical_not(is_dest))
    def _():
        pl.semaphore_wait(barrier, 22)

    corner = remote(l1_hbm.at[0, 0], kbuf, ksend, krecv, home, q)
    corner_here = pltpu.make_async_copy(l1_hbm.at[0, 0], kbuf, krecv)

    @pl.when(jnp.logical_and(p == 0, jnp.logical_not(is_dest)))
    def _():
        corner.start()

    @pl.when(jnp.logical_and(p == 0, is_dest))
    def _():
        corner_here.start()

    def swap_whole(n):
        return remote(pbuf.at[n], xbuf.at[n], xsend.at[n], xrecv.at[n], 2 * z + cd, q)

    def swap_half(n):
        rows = pl.ds(pl.multiple_of((1 - c) * HALF, HALF), HALF)
        return remote(
            pbuf.at[n, rows], xbuf.at[n, pl.ds(0, HALF)], xsend.at[n], xrecv.at[n], 2 * z + 1 - c, q
        )

    def products(i):
        col = (i + 1) % 4
        load_g(col).wait()

        def halve(kb, _):
            hi, lo = split(gbuf[col, kb])
            at = pl.ds(pl.multiple_of(kb * B, B), B)
            ghi[at, :] = hi
            glo[at, :] = lo
            return 0

        lax.fori_loop(0, 8, halve, 0)

        def one(panel, _):
            rows = pl.ds(pl.multiple_of(panel * B, B), B)
            lh = lthi[rows, :]
            pbuf[4 * panel + i] = mm(lh, ghi[...]) + (mm(lh, glo[...]) + mm(ltlo[rows, :], ghi[...]))

            @pl.when(helper)
            def _():
                swap_whole(4 * panel + i).start()

            @pl.when(off_chip)
            def _():
                swap_half(4 * panel + i).start()

            return 0

        lax.fori_loop(0, 2, one, 0)

    def pass_on(n):
        last = pos == 2
        zn = jnp.where(c == 0, (z + 1) % 4, (z + 3) % 4)
        cn = jnp.where(last, cd, c)
        return remote(sbuf.at[n], cbuf.at[n, c], csend.at[n], crecv.at[n, c], 2 * zn + cn, q)

    def got_sum(n, half):
        return remote(cbuf.at[n, half], cbuf.at[n, half], csend.at[n], crecv.at[n, half], home, q)

    def chain(n):
        swap_half(n).wait_recv()
        rows = pl.ds(pl.multiple_of(c * HALF, HALF), HALF)
        sbuf[n] = pbuf[n, rows, :] + xbuf[n, 0:HALF, :]

        @pl.when(pos > 0)
        def _():
            got_sum(n, c).wait_recv()
            sbuf[n] += cbuf[n, c]

        pass_on(n).start()

    def whole_sum(n):
        swap_whole(n).wait_recv()
        got_sum(n, 0).wait_recv()
        got_sum(n, 1).wait_recv()
        xbuf[n] += pbuf[n]
        xbuf[n, 0:HALF, :] += cbuf[n, 0]
        xbuf[n, HALF:B, :] += cbuf[n, 1]
        return xbuf[n]

    def finish_two(n):
        col = (n + 1) % 4
        r = 2 * col + q // 8
        total = whole_sum(n)
        load_h(0, col).wait()
        resid = hbuf[0, col].T - 2.0 * total
        at = dot3(w2_ref[...].T, resid)
        obuf[0, r] = at.T
        dacc2[:, 0:16, :] += dot3(at, lbuf[0, r]).reshape(16, 16, B)
        dacc2[:, 16:32, :] += dot3(at, lbuf[1, r]).reshape(16, 16, B)
        zbuf[col] = SCALE * dot3(kbuf[...].T, at)

    def finish_one(n):
        col = (n + 1) % 4
        r = 2 * col + q // 8
        total = whole_sum(n)
        load_h(1, col).wait()
        resid = hbuf[1, col].T - 2.0 * total - zbuf[col]
        xbuf[n] = resid

        @pl.when(jnp.logical_and(is_root, n == 7))
        def _():
            def got(i, _):
                send_cross(i).wait_recv()
                return 0

            lax.fori_loop(1, 16, got, 0)
            xbuf[n] -= xfull[...].T

        at = dot3(w1_ref[...].T, xbuf[n])
        obuf[1, r] = at.T
        dacc1[...] += dot3(at, lbuf[1, r]).reshape(16, 16, B)

    def rows16(j):
        return pl.ds(pl.multiple_of(j * 16, 16), 16)

    def spread(rnd, j, me):
        src, dst = ((dacc2, rs2), (dacc1, rs1))[rnd]
        return remote(src.at[j], dst.at[me], rsend.at[rnd, j], rrecv.at[rnd, me], j % 8, j)

    def spread_all(rnd):
        def send(i, _):
            spread(rnd, (q + i) % 16, q).start()
            return 0

        lax.fori_loop(1, 16, send, 0)

    def send_cross(j):
        return remote(xfull.at[rows16(j)], xfull.at[rows16(j)], xxsend, xxrecv.at[j], 0, 0)

    def to_plane(rnd, i):
        mine = dfull.at[rnd, rows16(q)]
        return remote(mine, mine, bsend.at[rnd, i], drecv.at[rnd, q], p, (q + i) % 16)

    def own_rows(rnd):
        src, dst = ((dacc2, rs2), (dacc1, rs1))[rnd]

        def add(i, acc):
            j = (q + i) % 16
            spread(rnd, q, j).wait_recv()
            return acc + dst[j]

        total = lax.fori_loop(1, 16, add, src[q])
        dfull[rnd, rows16(q), :] = -SCALE * total[0:16]
        if rnd == 0:
            xfull[rows16(q), :] = SCALE * total[16:32]

            @pl.when(jnp.logical_not(is_root))
            def _():
                send_cross(q).start()

        def send(i, _):
            to_plane(rnd, i).start()
            return 0

        lax.fori_loop(1, 16, send, 0)

    def slice_copy(rnd, j, i):
        here = dfull.at[rnd, rows16(j)]
        return remote(here, here, vsend.at[rnd, j // 8, i], drecv.at[rnd, j], (p + i) % 8, q)

    def to_column(rnd):
        for h in range(2):
            j = p + 8 * h

            @pl.when(j != q)
            def _(j=j):
                slice_copy(rnd, j, 0).wait_recv()

            def send(i, _, j=j):
                slice_copy(rnd, j, i).start()
                return 0

            lax.fori_loop(1, 8, send, 0)

    flows = []
    for h in range(2):
        qs = p + 8 * h
        dx = (x - qs % 4 + 4) % 4
        dy = (y - qs // 4 + 4) % 4
        for turn_by in range(4):
            u, v = ((dx, dy), (dy, (4 - dx) % 4), ((4 - dx) % 4, (4 - dy) % 4), ((4 - dy) % 4, dx))[turn_by]
            flows.append((h, turn_by, lookup(CHILDREN, 4 * u + v), lookup(DEPTH, 4 * u + v)))
    sides = (4 * y + (x + 1) % 4, 4 * ((y + 1) % 4) + x, 4 * y + (x + 3) % 4, 4 * ((y + 3) % 4) + x)

    def tile_part(n, f):
        h, turn_by, _, _ = flows[f]
        return obuf.at[n // 4, 2 * ((n + 1) % 4) + h, pl.ds(QUARTER * turn_by, QUARTER), :]

    def branch(n, f, e):
        part = tile_part(n, f)
        return remote(
            part, part, tsend.at[n % 2, f, e], trecv.at[n, f], p, sides[(e + flows[f][1]) % 4]
        )

    def has_branch(f, e):
        return (flows[f][2] // (1 << e)) % 2 == 1

    def store(n, f):
        h, turn_by, _, _ = flows[f]
        r = 2 * ((n + 1) % 4) + h
        rows = pl.ds(QUARTER * turn_by, QUARTER)

        @pl.when(n < 4)
        def _():
            pltpu.make_async_copy(tile_part(n, f), a2_hbm.at[r, 0, rows, :], osem.at[0]).start()

        @pl.when(n >= 4)
        def _():
            pltpu.make_async_copy(tile_part(n, f), a1_hbm.at[r, 0, rows, :], osem.at[1]).start()

    def forward(t, f):
        depth = flows[f][3]
        n = t - 4 - depth

        @pl.when(jnp.logical_and(n >= 0, n < BLOCKS))
        def _():
            @pl.when(depth > 0)
            def _():
                branch(n, f, 0).wait_recv()

            for e in range(4):
                @pl.when(has_branch(f, e))
                def _(e=e):
                    @pl.when(n >= 2)
                    def _():
                        branch(n - 2, f, e).wait_send()

                    branch(n, f, e).start()

            store(n, f)

    def step(t, _):
        @pl.when(t < 4)
        def _():
            products(t)

        ahead = t - 1 - pos

        @pl.when(jnp.logical_and(off_chip, jnp.logical_and(ahead >= 0, ahead < BLOCKS)))
        def _():
            chain(ahead)

        @pl.when(is_dest)
        def _():
            @pl.when(t == 4)
            def _():
                dacc2[...] = jnp.zeros_like(dacc2)
                dacc1[...] = jnp.zeros_like(dacc1)
                corner_here.wait()

            @pl.when(t == 8)
            def _():
                own_rows(0)

            @pl.when(t == 12)
            def _():
                own_rows(1)

            @pl.when(jnp.logical_and(t >= 4, t < 8))
            def _():
                finish_two(t - 4)

            @pl.when(t == 7)
            def _():
                spread_all(0)

            @pl.when(jnp.logical_and(t >= 8, t < 12))
            def _():
                finish_one(t - 4)

            @pl.when(t == 11)
            def _():
                spread_all(1)

        @pl.when(t == 10)
        def _():
            to_column(0)

        @pl.when(t == 13)
        def _():
            to_column(1)

        for f in range(8):
            forward(t, f)
        return 0

    lax.fori_loop(0, STEPS, step, 0)

    for rnd, out in ((0, d2_hbm), (1, d1_hbm)):
        for h in range(2):
            def late(i, _, rnd=rnd, h=h):
                slice_copy(rnd, (p + i) % 8 + 8 * h, 0).wait_recv()
                return 0

            lax.fori_loop(1, 8, late, 0)
        pltpu.make_async_copy(dfull.at[rnd], out, osem.at[2 + rnd]).start()

    def sent(n, _):
        @pl.when(helper)
        def _():
            swap_whole(n).wait_send()

        @pl.when(off_chip)
        def _():
            swap_half(n).wait_send()
            pass_on(n).wait_send()

        return 0

    lax.fori_loop(0, BLOCKS, sent, 0)

    @pl.when(jnp.logical_and(p == 0, jnp.logical_not(is_dest)))
    def _():
        corner.wait_send()

    for f in range(8):
        for e in range(4):
            @pl.when(has_branch(f, e))
            def _(f=f, e=e):
                branch(6, f, e).wait_send()
                branch(7, f, e).wait_send()

    for rnd in range(2):
        for h in range(2):
            def column_sent(i, _, rnd=rnd, h=h):
                slice_copy(rnd, p + 8 * h, i).wait_send()
                return 0

            lax.fori_loop(1, 8, column_sent, 0)

        @pl.when(is_dest)
        def _(rnd=rnd):
            def home_sent(i, _):
                spread(rnd, (q + i) % 16, q).wait_send()
                to_plane(rnd, i).wait_send()
                return 0

            lax.fori_loop(1, 16, home_sent, 0)

    @pl.when(jnp.logical_and(is_dest, jnp.logical_not(is_root)))
    def _():
        send_cross(q).wait_send()

    pltpu.make_async_copy(obuf.at[0], a2_hbm.at[:, 0], osem.at[0]).wait()
    pltpu.make_async_copy(obuf.at[1], a1_hbm.at[:, 0], osem.at[1]).wait()
    pltpu.make_async_copy(dfull.at[0], d2_hbm, osem.at[2]).wait()
    pltpu.make_async_copy(dfull.at[1], d1_hbm, osem.at[3]).wait()


def local(grad_trailing, panel_one, panel_two, grad_one, grad_two, inv_one, inv_two):
    any_space = pl.BlockSpec(memory_space=pl.ANY)
    vmem = pl.BlockSpec(memory_space=pltpu.VMEM)
    panel = jax.ShapeDtypeStruct(panel_one.shape, F32)
    square = jax.ShapeDtypeStruct((B, B), F32)
    dma = pltpu.SemaphoreType.DMA
    return pl.pallas_call(
        kernel,
        out_shape=(panel, panel, square, square),
        in_specs=[any_space] * 5 + [vmem] * 2,
        out_specs=(any_space,) * 4,
        scratch_shapes=[
            pltpu.VMEM((4, 8, B, B), F32),
            pltpu.VMEM((8 * B, B), BF16),
            pltpu.VMEM((8 * B, B), BF16),
            pltpu.VMEM((2, 8, B, B), F32),
            pltpu.VMEM((2 * B, 8 * B), BF16),
            pltpu.VMEM((2 * B, 8 * B), BF16),
            pltpu.VMEM((2, 4, B, B), F32),
            pltpu.VMEM((B, B), F32),
            pltpu.VMEM((4, B, B), F32),
            pltpu.VMEM((BLOCKS, B, B), F32),
            pltpu.VMEM((BLOCKS, B, B), F32),
            pltpu.VMEM((BLOCKS, 2, HALF, B), F32),
            pltpu.VMEM((BLOCKS, HALF, B), F32),
            pltpu.VMEM((2, 8, B, B), F32),
            pltpu.VMEM((16, 32, B), F32),
            pltpu.VMEM((16, 16, B), F32),
            pltpu.VMEM((16, 32, B), F32),
            pltpu.VMEM((16, 16, B), F32),
            pltpu.VMEM((2, B, B), F32),
            pltpu.VMEM((B, B), F32),
            dma((4,)),
            dma((2,)),
            dma((2, 4)),
            dma,
            dma,
            dma((BLOCKS,)),
            dma((BLOCKS,)),
            dma((BLOCKS,)),
            dma((BLOCKS, 2)),
            dma((2, 8, 4)),
            dma((BLOCKS, 8)),
            dma((4,)),
            dma((2, 16)),
            dma((2, 16)),
            dma((2, 16)),
            dma((2, 16)),
            dma((2, 2, 8)),
            dma,
            dma((16,)),
        ],
        compiler_params=pltpu.CompilerParams(
            collective_id=0, has_side_effects=True, vmem_limit_bytes=56 * 2**20
        ),
        cost_estimate=pl.CostEstimate(flops=7_000_000_000, bytes_accessed=22_000_000, transcendentals=0),
    )(grad_trailing, panel_one, panel_two, grad_one, grad_two, inv_one, inv_two)


def solution(mesh):
    placed = (
        P(None, "prow", None, None, "pcol", None),
        P(None, "prow", None, None),
        P(None, "prow", None, None),
        P(None, "prow", None, None),
        P(None, "prow", None, None),
        P(),
        P(),
    )
    return jax.shard_map(
        local,
        mesh=mesh,
        in_specs=placed,
        out_specs=(P(None, "prow", None, None), P(None, "prow", None, None), P(), P()),
        check_vma=False,
    )
```

profile of v0, /device:TPU:2, one launch (start us, length us, event | category | flops | bytes accessed | tf_op | source)
XLA Modules:
  0.0 90.6 jit_solution(14761199490894658903)
XLA Ops:
  0.6 84.0 %shard_map.102 = (f32[8,1,256,256]{3,2,1,0:T(8,128)}, f32[8,1,256,256]{3,2,1,0:T(8,128)}, f32[256,256]{1,0:T(8,128)}, f32[256,256]{1,0:T(8,128)}) custom-call(f32[8,1,256,4,1,256]{5,4,3,2,1,0:T(1,128)} %g_hbm.1, f32[8,1,256,256]{3,2,1,0:T(8,128)} %l1_hbm.1, f32[8,1,256,256]{3,2,1,0:T(8,128)} %l2_hbm.1, f32[8,1,256,256]{3,2,1,0:T(8,128)} %h1_hbm.1, ...), custom_call_target="tpu_custom_call" | custom-call | flops 7000000000 | bytes 22000000 | tf_op jit(solution)/shard_map/pallas_call | solution.py:503
  84.6 0.0 copy-start
  84.6 3.2 %copy.15 = f32[8,1,256,256]{3,2,1,0:T(8,128)} copy(f32[8,1,256,256]{3,2,1,0:T(8,128)} %get-tuple-element.8) | data formatting | bytes 4194304
  87.8 0.0 copy-done
  87.8 0.0 copy-start.2
  87.8 0.0 copy-start.1
  87.8 1.3 %copy.16 = f32[8,1,256,256]{3,2,1,0:T(8,128)} copy(f32[8,1,256,256]{3,2,1,0:T(8,128)S(1)} %copy-done) | data formatting | bytes 4194304
  89.1 0.0 copy-done.2
  89.2 0.7 copy.17
  89.9 0.0 copy-done.1
  89.9 0.7 copy.18
Async XLA Ops:
  84.6 3.2 %copy-start = (f32[8,1,256,256]{3,2,1,0:T(8,128)S(1)}, f32[8,1,256,256]{3,2,1,0:T(8,128)}, u32[]{:S(2)}) copy-start(f32[8,1,256,256]{3,2,1,0:T(8,128)} %get-tuple-element.9) | copy-start | bytes 6291460
  87.8 1.3 %copy-start.2 = (f32[256,256]{1,0:T(8,128)S(1)}, f32[256,256]{1,0:T(8,128)}, u32[]{:S(2)}) copy-start(f32[256,256]{1,0:T(8,128)} %get-tuple-element.10) | copy-start | bytes 786436
  87.8 2.0 %copy-start.1 = (f32[256,256]{1,0:T(8,128)S(1)}, f32[256,256]{1,0:T(8,128)}, u32[]{:S(2)}) copy-start(f32[256,256]{1,0:T(8,128)} %get-tuple-element.11) | copy-start | bytes 786436
where the time goes:
time: 90.7 us; the launch traced here: 90.6 us
  Pallas kernels  84 us (93%)
  local copies, waits for them, and re-layouts  5.93 us (7%)
    pallas_call x1, Pallas kernels, local(): pl.pallas_call(kernel, out_shape=(panel, panel, square, square), in_specs...  84 us
    unnamed x10, local copies, waits for them, and re-layouts  5.93 us

commit v1 on v0

--- a/solution.py
+++ b/solution.py
@@ -19,7 +19,11 @@
 DEPTH = (0, 3, 4, 3, 1, 2, 3, 2, 2, 3, 4, 3, 3, 4, 5, 4)
 DEEPEST = max(DEPTH)
 BLOCKS = 8
-STEPS = BLOCKS + 4 + DEEPEST
+HOP = 4
+START = 1 + 3 * HOP
+TREE = 2
+STEPS = START + BLOCKS + TREE * DEEPEST
+FINISHED = (1, 2, 4, 6, 7, 7, 8)
 
 
 def split(value):
@@ -47,7 +51,7 @@
 def kernel(
     g_hbm, l1_hbm, l2_hbm, h1_hbm, h2_hbm, w1_ref, w2_ref,
     a1_hbm, a2_hbm, d1_hbm, d2_hbm,
-    gbuf, ghi, glo, lbuf, lthi, ltlo, hbuf, kbuf, zbuf, pbuf, xbuf, cbuf, sbuf, obuf,
+    gbuf, ghi, glo, turned_hi, turned_lo, lbuf, lthi, ltlo, hbuf, kbuf, zbuf, pbuf, xbuf, cbuf, sbuf, obuf,
     dacc2, dacc1, rs2, rs1, dfull, xfull,
     gsem, lsem, hsem, ksend, krecv, xsend, xrecv, csend, crecv, tsend, trecv, osem,
     rsend, rrecv, bsend, drecv, vsend, xxsend, xxrecv,
@@ -164,35 +168,34 @@
             pbuf.at[n, rows], xbuf.at[n, pl.ds(0, HALF)], xsend.at[n], xrecv.at[n], 2 * z + 1 - c, q
         )
 
-    def products(i):
-        col = (i + 1) % 4
-        load_g(col).wait()
-
-        def halve(kb, _):
-            hi, lo = split(gbuf[col, kb])
-            at = pl.ds(pl.multiple_of(kb * B, B), B)
-            ghi[at, :] = hi
-            glo[at, :] = lo
-            return 0
-
-        lax.fori_loop(0, 8, halve, 0)
-
-        def one(panel, _):
-            rows = pl.ds(pl.multiple_of(panel * B, B), B)
-            lh = lthi[rows, :]
-            pbuf[4 * panel + i] = mm(lh, ghi[...]) + (mm(lh, glo[...]) + mm(ltlo[rows, :], ghi[...]))
-
-            @pl.when(helper)
-            def _():
-                swap_whole(4 * panel + i).start()
-
-            @pl.when(off_chip)
-            def _():
-                swap_half(4 * panel + i).start()
-
-            return 0
-
-        lax.fori_loop(0, 2, one, 0)
+    def products(n):
+        col = (n + 1) % 4
+        panel = n // 4
+
+        @pl.when(n < 4)
+        def _():
+            load_g(col).wait()
+
+            def halve(kb, _):
+                hi, lo = split(gbuf[col, kb])
+                at = pl.ds(pl.multiple_of(kb * B, B), B)
+                ghi[col, at, :] = hi
+                glo[col, at, :] = lo
+                return 0
+
+            lax.fori_loop(0, 8, halve, 0)
+
+        rows = pl.ds(pl.multiple_of(panel * B, B), B)
+        lh = lthi[rows, :]
+        pbuf[n] = mm(lh, ghi[col]) + (mm(lh, glo[col]) + mm(ltlo[rows, :], ghi[col]))
+
+        @pl.when(helper)
+        def _():
+            swap_whole(n).start()
+
+        @pl.when(off_chip)
+        def _():
+            swap_half(n).start()
 
     def pass_on(n):
         last = pos == 2
@@ -224,17 +227,27 @@
         xbuf[n, HALF:B, :] += cbuf[n, 1]
         return xbuf[n]
 
+    def keep_turned(i, value):
+        hi, lo = split(value.T)
+        turned_hi[i] = hi
+        turned_lo[i] = lo
+
+    def turned_dot3(i, right):
+        rh, rl = split(right)
+        lh = turned_hi[i]
+        return mm(lh, rh) + (mm(lh, rl) + mm(turned_lo[i], rh))
+
     def finish_two(n):
         col = (n + 1) % 4
         r = 2 * col + q // 8
         total = whole_sum(n)
         load_h(0, col).wait()
         resid = hbuf[0, col].T - 2.0 * total
-        at = dot3(w2_ref[...].T, resid)
+        at = turned_dot3(0, resid)
         obuf[0, r] = at.T
         dacc2[:, 0:16, :] += dot3(at, lbuf[0, r]).reshape(16, 16, B)
         dacc2[:, 16:32, :] += dot3(at, lbuf[1, r]).reshape(16, 16, B)
-        zbuf[col] = SCALE * dot3(kbuf[...].T, at)
+        zbuf[col] = SCALE * turned_dot3(2, at)
 
     def finish_one(n):
         col = (n + 1) % 4
@@ -253,7 +266,7 @@
             lax.fori_loop(1, 16, got, 0)
             xbuf[n] -= xfull[...].T
 
-        at = dot3(w1_ref[...].T, xbuf[n])
+        at = turned_dot3(1, xbuf[n])
         obuf[1, r] = at.T
         dacc1[...] += dot3(at, lbuf[1, r]).reshape(16, 16, B)
 
@@ -357,7 +370,7 @@
 
     def forward(t, f):
         depth = flows[f][3]
-        n = t - 4 - depth
+        n = t - START - TREE * depth
 
         @pl.when(jnp.logical_and(n >= 0, n < BLOCKS))
         def _():
@@ -377,53 +390,68 @@
             store(n, f)
 
     def step(t, _):
-        @pl.when(t < 4)
+        @pl.when(t < BLOCKS)
         def _():
             products(t)
 
-        ahead = t - 1 - pos
+        ahead = t - 1 - HOP * pos
 
         @pl.when(jnp.logical_and(off_chip, jnp.logical_and(ahead >= 0, ahead < BLOCKS)))
         def _():
             chain(ahead)
 
+        since = t - START
+
         @pl.when(is_dest)
         def _():
-            @pl.when(t == 4)
+            @pl.when(since == -1)
             def _():
                 dacc2[...] = jnp.zeros_like(dacc2)
                 dacc1[...] = jnp.zeros_like(dacc1)
+                keep_turned(0, w2_ref[...])
+                keep_turned(1, w1_ref[...])
                 corner_here.wait()
-
-            @pl.when(t == 8)
+                keep_turned(2, kbuf[...])
+
+            @pl.when(since == 4)
             def _():
                 own_rows(0)
 
-            @pl.when(t == 12)
+            @pl.when(since == 8)
             def _():
                 own_rows(1)
 
-            @pl.when(jnp.logical_and(t >= 4, t < 8))
-            def _():
-                finish_two(t - 4)
-
-            @pl.when(t == 7)
+            def finish(n, _):
+                @pl.when(n < 4)
+                def _():
+                    finish_two(n)
+
+                @pl.when(n >= 4)
+                def _():
+                    finish_one(n)
+
+                return 0
+
+            done = jnp.where(since < len(FINISHED), lookup(FINISHED, since), BLOCKS)
+            before = lookup((0,) + FINISHED, since)
+
+            @pl.when(jnp.logical_and(since >= 0, since < len(FINISHED)))
+            def _():
+                lax.fori_loop(before, done, finish, 0)
+
+            @pl.when(since == 2)
             def _():
                 spread_all(0)
 
-            @pl.when(jnp.logical_and(t >= 8, t < 12))
-            def _():
-                finish_one(t - 4)
-
-            @pl.when(t == 11)
+            @pl.when(since == 6)
             def _():
                 spread_all(1)
 
-        @pl.when(t == 10)
+        @pl.when(since == 7)
         def _():
             to_column(0)
 
-        @pl.when(t == 13)
+        @pl.when(since == 11)
         def _():
             to_column(1)
 
@@ -494,21 +522,32 @@
     pltpu.make_async_copy(dfull.at[1], d1_hbm, osem.at[3]).wait()
 
 
+def hand_over(*refs):
+    sems = refs[8]
+    copies = [pltpu.make_async_copy(refs[i], refs[4 + i], sems.at[i]) for i in range(4)]
+    for copy in copies:
+        copy.start()
+    for copy in copies:
+        copy.wait()
+
+
 def local(grad_trailing, panel_one, panel_two, grad_one, grad_two, inv_one, inv_two):
     any_space = pl.BlockSpec(memory_space=pl.ANY)
     vmem = pl.BlockSpec(memory_space=pltpu.VMEM)
     panel = jax.ShapeDtypeStruct(panel_one.shape, F32)
     square = jax.ShapeDtypeStruct((B, B), F32)
     dma = pltpu.SemaphoreType.DMA
-    return pl.pallas_call(
+    results = pl.pallas_call(
         kernel,
         out_shape=(panel, panel, square, square),
         in_specs=[any_space] * 5 + [vmem] * 2,
         out_specs=(any_space,) * 4,
         scratch_shapes=[
             pltpu.VMEM((4, 8, B, B), F32),
-            pltpu.VMEM((8 * B, B), BF16),
-            pltpu.VMEM((8 * B, B), BF16),
+            pltpu.VMEM((4, 8 * B, B), BF16),
+            pltpu.VMEM((4, 8 * B, B), BF16),
+            pltpu.VMEM((3, B, B), BF16),
+            pltpu.VMEM((3, B, B), BF16),
             pltpu.VMEM((2, 8, B, B), F32),
             pltpu.VMEM((2 * B, 8 * B), BF16),
             pltpu.VMEM((2 * B, 8 * B), BF16),
@@ -551,6 +590,13 @@
         ),
         cost_estimate=pl.CostEstimate(flops=7_000_000_000, bytes_accessed=22_000_000, transcendentals=0),
     )(grad_trailing, panel_one, panel_two, grad_one, grad_two, inv_one, inv_two)
+    return pl.pallas_call(
+        hand_over,
+        out_shape=(panel, panel, square, square),
+        in_specs=[any_space] * 4,
+        out_specs=(any_space,) * 4,
+        scratch_shapes=[dma((4,))],
+    )(*results)
 
 
 def solution(mesh):

time: 90.7 us -> 220 us (2.43)
  Pallas kernels: 84 us -> 220 us
  local copies, waits for them, and re-layouts: 5.93 us -> 0 us
    pallas_call x0 -> x1, Pallas kernels: none -> 144 us  [local(): pl.pallas_call(hand_over, out_shape=(panel, panel, square, square), in_sp...]
    pallas_call x1, Pallas kernels: 84 us -> 75.5 us  [local(): pl.pallas_call(kernel, out_shape=(panel, panel, square, square), in_specs...]
    unnamed x10 -> x0, local copies, waits for them, and re-layouts: 5.93 us -> none
where the time goes in v1:
time: 220 us
  Pallas kernels  220 us (100%)
    pallas_call x1, Pallas kernels, local(): pl.pallas_call(hand_over, out_shape=(panel, panel, square, square), in_sp...  144 us
    pallas_call x1, Pallas kernels, local(): pl.pallas_call(kernel, out_shape=(panel, panel, square, square), in_specs...  75.5 us

profile of v1, /device:TPU:2, one launch (start us, length us, event | category | flops | bytes accessed | tf_op | source)
XLA Modules:
  0.0 220.2 jit_solution(9706840463167638254)
XLA Ops:
  0.6 75.5 %shard_map.102 = (f32[8,1,256,256]{3,2,1,0:T(8,128)}, f32[8,1,256,256]{3,2,1,0:T(8,128)}, f32[256,256]{1,0:T(8,128)}, f32[256,256]{1,0:T(8,128)}) custom-call(f32[8,1,256,4,1,256]{5,4,3,2,1,0:T(1,128)} %g_hbm.1, f32[8,1,256,256]{3,2,1,0:T(8,128)} %l1_hbm.1, f32[8,1,256,256]{3,2,1,0:T(8,128)} %l2_hbm.1, f32[8,1,256,256]{3,2,1,0:T(8,128)} %h1_hbm.1, ...), custom_call_target="tpu_custom_call" | custom-call | flops 7000000000 | bytes 22000000 | tf_op jit(solution)/shard_map/pallas_call | solution.py:540
  76.1 144.1 %shard_map.103 = (f32[8,1,256,256]{3,2,1,0:T(8,128)}, f32[8,1,256,256]{3,2,1,0:T(8,128)}, f32[256,256]{1,0:T(8,128)}, f32[256,256]{1,0:T(8,128)}) custom-call(f32[8,1,256,256]{3,2,1,0:T(8,128)} %get-tuple-element.8.refs_0_, f32[8,1,256,256]{3,2,1,0:T(8,128)} %get-tuple-element.9.refs_1_, f32[256,256]{1,0:T(8,128)} %get-tuple-element.10.refs_2_, ...), custom_call_target="tpu_custom_call" | custom-call | tf_op jit(solution)/shard_map/pallas_call | solution.py:593

commit v2 on v1

--- a/solution.py
+++ b/solution.py
@@ -19,11 +19,15 @@
 DEPTH = (0, 3, 4, 3, 1, 2, 3, 2, 2, 3, 4, 3, 3, 4, 5, 4)
 DEEPEST = max(DEPTH)
 BLOCKS = 8
-HOP = 4
+HOP = 3
 START = 1 + 3 * HOP
 TREE = 2
-STEPS = START + BLOCKS + TREE * DEEPEST
-FINISHED = (1, 2, 4, 6, 7, 7, 8)
+FINISHED = (1, 3, 4, 6, 7, 7, 7, 8)
+SPREAD = (2, 7)
+OWN = (5, 10)
+COLUMN = (8, 13)
+LAST = BLOCKS - 1 + TREE * DEEPEST
+NEVER = 1 << 20
 
 
 def split(value):
@@ -51,10 +55,10 @@
 def kernel(
     g_hbm, l1_hbm, l2_hbm, h1_hbm, h2_hbm, w1_ref, w2_ref,
     a1_hbm, a2_hbm, d1_hbm, d2_hbm,
-    gbuf, ghi, glo, turned_hi, turned_lo, lbuf, lthi, ltlo, hbuf, kbuf, zbuf, pbuf, xbuf, cbuf, sbuf, obuf,
+    gbuf, ghi, glo, turned_hi, turned_lo, lbuf, lthi, ltlo, hbuf, kbuf, zbuf, pbuf, xbuf, cbuf, sbuf, obuf, atbuf,
     dacc2, dacc1, rs2, rs1, dfull, xfull,
     gsem, lsem, hsem, ksend, krecv, xsend, xrecv, csend, crecv, tsend, trecv, osem,
-    rsend, rrecv, bsend, drecv, vsend, xxsend, xxrecv,
+    rsend, rrecv, bsend, brecv, drecv, vsend, xxsend, xxrecv,
 ):
     p = lax.axis_index("prow")
     q = lax.axis_index("pcol")
@@ -97,6 +101,20 @@
             for i in range(4):
                 load_h(panel, (i + 1) % 4).start()
 
+    flows = []
+    for h in range(2):
+        qs = p + 8 * h
+        dx = (x - qs % 4 + 4) % 4
+        dy = (y - qs // 4 + 4) % 4
+        for turn_by in range(4):
+            u, v = ((dx, dy), (dy, (4 - dx) % 4), ((4 - dx) % 4, (4 - dy) % 4), ((4 - dy) % 4, dx))[turn_by]
+            children = lookup(CHILDREN, 4 * u + v)
+            depth = lookup(DEPTH, 4 * u + v)
+            has = [(children // (1 << e)) % 2 == 1 for e in range(4)]
+            first = jnp.where(children > 0, TREE * depth, NEVER)
+            flows.append((turn_by, has, depth > 0, first, children > 0))
+    sides = (4 * y + (x + 1) % 4, 4 * ((y + 1) % 4) + x, 4 * y + (x + 3) % 4, 4 * ((y + 3) % 4) + x)
+
     barrier = pltpu.get_barrier_semaphore()
 
     def greet(pp, qq):
@@ -128,10 +146,10 @@
     def _():
         lax.fori_loop(1, 16, greet_dest, 0)
 
-    for panel in range(2):
+    def turn_panel(panel):
         load_l(panel).wait()
 
-        def turn(kb, _, panel=panel):
+        def turn(kb, _):
             hi, lo = split(lbuf[panel, kb].T)
             at = pl.ds(pl.multiple_of(kb * B, B), B)
             lthi[panel * B:(panel + 1) * B, at] = hi
@@ -139,6 +157,8 @@
             return 0
 
         lax.fori_loop(0, 8, turn, 0)
+
+    turn_panel(0)
 
     @pl.when(is_dest)
     def _():
@@ -244,7 +264,13 @@
         load_h(0, col).wait()
         resid = hbuf[0, col].T - 2.0 * total
         at = turned_dot3(0, resid)
-        obuf[0, r] = at.T
+        obuf[pl.ds(8 * n + 4 * (q // 8), 4)] = at.T.reshape(4, QUARTER, B)
+        atbuf[n] = at
+
+    def sums_two(n):
+        col = (n + 1) % 4
+        r = 2 * col + q // 8
+        at = atbuf[n]
         dacc2[:, 0:16, :] += dot3(at, lbuf[0, r]).reshape(16, 16, B)
         dacc2[:, 16:32, :] += dot3(at, lbuf[1, r]).reshape(16, 16, B)
         zbuf[col] = SCALE * turned_dot3(2, at)
@@ -260,22 +286,28 @@
         @pl.when(jnp.logical_and(is_root, n == 7))
         def _():
             def got(i, _):
-                send_cross(i).wait_recv()
+                cross_rows(i).wait_recv()
                 return 0
 
             lax.fori_loop(1, 16, got, 0)
             xbuf[n] -= xfull[...].T
 
         at = turned_dot3(1, xbuf[n])
-        obuf[1, r] = at.T
-        dacc1[...] += dot3(at, lbuf[1, r]).reshape(16, 16, B)
+        obuf[pl.ds(8 * n + 4 * (q // 8), 4)] = at.T.reshape(4, QUARTER, B)
+        atbuf[n] = at
+
+    def sums_one(n):
+        r = 2 * ((n + 1) % 4) + q // 8
+        dacc1[...] += dot3(atbuf[n], lbuf[1, r]).reshape(16, 16, B)
 
     def rows16(j):
-        return pl.ds(pl.multiple_of(j * 16, 16), 16)
+        return pl.ds(pl.multiple_of((2 * (j % 8) + j // 8) * 16, 16), 16)
 
     def spread(rnd, j, me):
         src, dst = ((dacc2, rs2), (dacc1, rs1))[rnd]
-        return remote(src.at[j], dst.at[me], rsend.at[rnd, j], rrecv.at[rnd, me], j % 8, j)
+        return remote(
+            src.at[2 * (j % 8) + j // 8], dst.at[me], rsend.at[rnd, j], rrecv.at[rnd, me], j % 8, j
+        )
 
     def spread_all(rnd):
         def send(i, _):
@@ -284,12 +316,12 @@
 
         lax.fori_loop(1, 16, send, 0)
 
-    def send_cross(j):
+    def cross_rows(j):
         return remote(xfull.at[rows16(j)], xfull.at[rows16(j)], xxsend, xxrecv.at[j], 0, 0)
 
-    def to_plane(rnd, i):
-        mine = dfull.at[rnd, rows16(q)]
-        return remote(mine, mine, bsend.at[rnd, i], drecv.at[rnd, q], p, (q + i) % 16)
+    def to_plane(rnd, i, h):
+        mine = dfull.at[rnd, rows16(p + 8 * h)]
+        return remote(mine, mine, bsend.at[rnd, i], brecv.at[rnd, h], p, (q + i) % 16)
 
     def own_rows(rnd):
         src, dst = ((dacc2, rs2), (dacc1, rs1))[rnd]
@@ -299,175 +331,195 @@
             spread(rnd, q, j).wait_recv()
             return acc + dst[j]
 
-        total = lax.fori_loop(1, 16, add, src[q])
+        total = lax.fori_loop(1, 16, add, src[2 * (q % 8) + q // 8])
         dfull[rnd, rows16(q), :] = -SCALE * total[0:16]
         if rnd == 0:
             xfull[rows16(q), :] = SCALE * total[16:32]
 
             @pl.when(jnp.logical_not(is_root))
             def _():
-                send_cross(q).start()
+                cross_rows(q).start()
 
         def send(i, _):
-            to_plane(rnd, i).start()
+            to_plane(rnd, i, q // 8).start()
             return 0
 
         lax.fori_loop(1, 16, send, 0)
 
-    def slice_copy(rnd, j, i):
-        here = dfull.at[rnd, rows16(j)]
-        return remote(here, here, vsend.at[rnd, j // 8, i], drecv.at[rnd, j], (p + i) % 8, q)
+    def pair_rows(rnd, pp, i):
+        here = dfull.at[rnd, pl.ds(pl.multiple_of(pp * 32, 32), 32)]
+        return remote(here, here, vsend.at[rnd, i], drecv.at[rnd, pp], (p + i) % 8, q)
 
     def to_column(rnd):
         for h in range(2):
-            j = p + 8 * h
-
-            @pl.when(j != q)
-            def _(j=j):
-                slice_copy(rnd, j, 0).wait_recv()
-
-            def send(i, _, j=j):
-                slice_copy(rnd, j, i).start()
-                return 0
-
-            lax.fori_loop(1, 8, send, 0)
-
-    flows = []
-    for h in range(2):
-        qs = p + 8 * h
-        dx = (x - qs % 4 + 4) % 4
-        dy = (y - qs // 4 + 4) % 4
-        for turn_by in range(4):
-            u, v = ((dx, dy), (dy, (4 - dx) % 4), ((4 - dx) % 4, (4 - dy) % 4), ((4 - dy) % 4, dx))[turn_by]
-            flows.append((h, turn_by, lookup(CHILDREN, 4 * u + v), lookup(DEPTH, 4 * u + v)))
-    sides = (4 * y + (x + 1) % 4, 4 * ((y + 1) % 4) + x, 4 * y + (x + 3) % 4, 4 * ((y + 3) % 4) + x)
-
-    def tile_part(n, f):
-        h, turn_by, _, _ = flows[f]
-        return obuf.at[n // 4, 2 * ((n + 1) % 4) + h, pl.ds(QUARTER * turn_by, QUARTER), :]
+            @pl.when(p + 8 * h != q)
+            def _(h=h):
+                to_plane(rnd, 1, h).wait_recv()
+
+        def send(i, _):
+            pair_rows(rnd, p, i).start()
+            return 0
+
+        lax.fori_loop(1, 8, send, 0)
 
     def branch(n, f, e):
-        part = tile_part(n, f)
+        part = obuf.at[8 * n + f]
         return remote(
-            part, part, tsend.at[n % 2, f, e], trecv.at[n, f], p, sides[(e + flows[f][1]) % 4]
+            part, part, tsend.at[n, f, e], trecv.at[8 * n + f], p, sides[(e + flows[f][0]) % 4]
         )
 
-    def has_branch(f, e):
-        return (flows[f][2] // (1 << e)) % 2 == 1
-
-    def store(n, f):
-        h, turn_by, _, _ = flows[f]
-        r = 2 * ((n + 1) % 4) + h
-        rows = pl.ds(QUARTER * turn_by, QUARTER)
-
-        @pl.when(n < 4)
-        def _():
-            pltpu.make_async_copy(tile_part(n, f), a2_hbm.at[r, 0, rows, :], osem.at[0]).start()
-
-        @pl.when(n >= 4)
-        def _():
-            pltpu.make_async_copy(tile_part(n, f), a1_hbm.at[r, 0, rows, :], osem.at[1]).start()
-
-    def forward(t, f):
-        depth = flows[f][3]
-        n = t - START - TREE * depth
+    def store(n):
+        for f in range(8):
+            @pl.when(jnp.logical_not(flows[f][4]))
+            def _(f=f):
+                branch(n, f, 0).wait_recv()
+
+        for h in range(2):
+            r = 2 * ((n + 1) % 4) + h
+            tile = obuf.at[pl.ds(8 * n + 4 * h, 4)]
+
+            @pl.when(n < 4)
+            def _(r=r, tile=tile):
+                pltpu.make_async_copy(tile, a2_hbm.at[r], osem.at[0]).start()
+
+            @pl.when(n >= 4)
+            def _(r=r, tile=tile):
+                pltpu.make_async_copy(tile, a1_hbm.at[r], osem.at[1]).start()
+
+    def forward(since, f):
+        _, has, below, first, _ = flows[f]
+        n = since - first
 
         @pl.when(jnp.logical_and(n >= 0, n < BLOCKS))
         def _():
-            @pl.when(depth > 0)
+            @pl.when(below)
             def _():
                 branch(n, f, 0).wait_recv()
 
             for e in range(4):
-                @pl.when(has_branch(f, e))
+                @pl.when(has[e])
                 def _(e=e):
-                    @pl.when(n >= 2)
-                    def _():
-                        branch(n - 2, f, e).wait_send()
-
                     branch(n, f, e).start()
 
-            store(n, f)
-
-    def step(t, _):
-        @pl.when(t < BLOCKS)
-        def _():
-            products(t)
-
+    def chain_turn(t):
         ahead = t - 1 - HOP * pos
 
         @pl.when(jnp.logical_and(off_chip, jnp.logical_and(ahead >= 0, ahead < BLOCKS)))
         def _():
             chain(ahead)
 
-        since = t - START
+    def columns(since):
+        for rnd in range(2):
+            @pl.when(since == COLUMN[rnd])
+            def _(rnd=rnd):
+                to_column(rnd)
+
+    def pass_all(since):
+        for f in range(8):
+            forward(since, f)
+
+    def produce(t, _):
+        products(t)
+
+        @pl.when(t == 3)
+        def _():
+            turn_panel(1)
+
+        chain_turn(t)
+        return 0
+
+    lax.fori_loop(0, BLOCKS, produce, 0)
+
+    def pass_sums(t, _):
+        chain_turn(t)
+        return 0
+
+    lax.fori_loop(BLOCKS, START, pass_sums, 0)
+
+    @pl.when(is_dest)
+    def _():
+        dacc2[...] = jnp.zeros_like(dacc2)
+        dacc1[...] = jnp.zeros_like(dacc1)
+        keep_turned(0, w2_ref[...])
+        keep_turned(1, w1_ref[...])
+        corner_here.wait()
+        keep_turned(2, kbuf[...])
+
+    def finish_step(since, _):
+        chain_turn(START + since)
+
+        def finish(n, _):
+            @pl.when(n < 4)
+            def _():
+                finish_two(n)
+
+            @pl.when(n >= 4)
+            def _():
+                finish_one(n)
+
+            return 0
+
+        def sums(n, _):
+            @pl.when(n < 4)
+            def _():
+                sums_two(n)
+
+            @pl.when(n >= 4)
+            def _():
+                sums_one(n)
+
+            return 0
+
+        before = lookup((0,) + FINISHED, since)
+        after = lookup(FINISHED, since)
 
         @pl.when(is_dest)
         def _():
-            @pl.when(since == -1)
-            def _():
-                dacc2[...] = jnp.zeros_like(dacc2)
-                dacc1[...] = jnp.zeros_like(dacc1)
-                keep_turned(0, w2_ref[...])
-                keep_turned(1, w1_ref[...])
-                corner_here.wait()
-                keep_turned(2, kbuf[...])
-
-            @pl.when(since == 4)
+            lax.fori_loop(before, after, finish, 0)
+
+        pass_all(since)
+
+        @pl.when(is_dest)
+        def _():
+            lax.fori_loop(before, after, sums, 0)
+
+            for rnd in range(2):
+                @pl.when(since == SPREAD[rnd])
+                def _(rnd=rnd):
+                    spread_all(rnd)
+
+            @pl.when(since == OWN[0])
             def _():
                 own_rows(0)
 
-            @pl.when(since == 8)
-            def _():
-                own_rows(1)
-
-            def finish(n, _):
-                @pl.when(n < 4)
-                def _():
-                    finish_two(n)
-
-                @pl.when(n >= 4)
-                def _():
-                    finish_one(n)
-
-                return 0
-
-            done = jnp.where(since < len(FINISHED), lookup(FINISHED, since), BLOCKS)
-            before = lookup((0,) + FINISHED, since)
-
-            @pl.when(jnp.logical_and(since >= 0, since < len(FINISHED)))
-            def _():
-                lax.fori_loop(before, done, finish, 0)
-
-            @pl.when(since == 2)
-            def _():
-                spread_all(0)
-
-            @pl.when(since == 6)
-            def _():
-                spread_all(1)
-
-        @pl.when(since == 7)
-        def _():
-            to_column(0)
-
-        @pl.when(since == 11)
-        def _():
-            to_column(1)
-
-        for f in range(8):
-            forward(t, f)
-        return 0
-
-    lax.fori_loop(0, STEPS, step, 0)
+        return 0
+
+    lax.fori_loop(0, len(FINISHED), finish_step, 0)
+
+    def last_step(since, _):
+        pass_all(since)
+
+        @pl.when(jnp.logical_and(is_dest, since == OWN[1]))
+        def _():
+            own_rows(1)
+
+        columns(since)
+        complete = since - TREE * DEEPEST
+
+        @pl.when(complete >= 0)
+        def _():
+            store(complete)
+
+        return 0
+
+    lax.fori_loop(len(FINISHED), LAST + 1, last_step, 0)
 
     for rnd, out in ((0, d2_hbm), (1, d1_hbm)):
-        for h in range(2):
-            def late(i, _, rnd=rnd, h=h):
-                slice_copy(rnd, (p + i) % 8 + 8 * h, 0).wait_recv()
-                return 0
-
-            lax.fori_loop(1, 8, late, 0)
+        def late(i, _, rnd=rnd):
+            pair_rows(rnd, (p + i) % 8, 0).wait_recv()
+            return 0
+
+        lax.fori_loop(1, 8, late, 0)
         pltpu.make_async_copy(dfull.at[rnd], out, osem.at[2 + rnd]).start()
 
     def sent(n, _):
@@ -490,56 +542,68 @@
 
     for f in range(8):
         for e in range(4):
-            @pl.when(has_branch(f, e))
+            @pl.when(flows[f][1][e])
             def _(f=f, e=e):
-                branch(6, f, e).wait_send()
-                branch(7, f, e).wait_send()
+                def part_sent(n, _):
+                    branch(n, f, e).wait_send()
+                    return 0
+
+                lax.fori_loop(0, BLOCKS, part_sent, 0)
 
     for rnd in range(2):
-        for h in range(2):
-            def column_sent(i, _, rnd=rnd, h=h):
-                slice_copy(rnd, p + 8 * h, i).wait_send()
-                return 0
-
-            lax.fori_loop(1, 8, column_sent, 0)
+        def column_sent(i, _, rnd=rnd):
+            pair_rows(rnd, p, i).wait_send()
+            return 0
+
+        lax.fori_loop(1, 8, column_sent, 0)
 
         @pl.when(is_dest)
         def _(rnd=rnd):
             def home_sent(i, _):
                 spread(rnd, (q + i) % 16, q).wait_send()
-                to_plane(rnd, i).wait_send()
+                to_plane(rnd, i, q // 8).wait_send()
                 return 0
 
             lax.fori_loop(1, 16, home_sent, 0)
 
     @pl.when(jnp.logical_and(is_dest, jnp.logical_not(is_root)))
     def _():
-        send_cross(q).wait_send()
-
-    pltpu.make_async_copy(obuf.at[0], a2_hbm.at[:, 0], osem.at[0]).wait()
-    pltpu.make_async_copy(obuf.at[1], a1_hbm.at[:, 0], osem.at[1]).wait()
+        cross_rows(q).wait_send()
+
+    pltpu.make_async_copy(a2_hbm, a2_hbm, osem.at[0]).wait()
+    pltpu.make_async_copy(a1_hbm, a1_hbm, osem.at[1]).wait()
     pltpu.make_async_copy(dfull.at[0], d2_hbm, osem.at[2]).wait()
     pltpu.make_async_copy(dfull.at[1], d1_hbm, osem.at[3]).wait()
 
 
-def hand_over(*refs):
-    sems = refs[8]
-    copies = [pltpu.make_async_copy(refs[i], refs[4 + i], sems.at[i]) for i in range(4)]
-    for copy in copies:
-        copy.start()
-    for copy in copies:
-        copy.wait()
+def hand_over(a1_in, a2_in, d1_in, d2_in, a1_out, a2_out, d1_out, d2_out, tiles, squares, sem_in, sem_out):
+    moves = []
+    for r in range(8):
+        moves.append((a1_in.at[r, 0], tiles.at[0, r], a1_out.at[r, 0]))
+        moves.append((a2_in.at[r, 0], tiles.at[1, r], a2_out.at[r, 0]))
+    moves.append((d1_in, squares.at[0], d1_out))
+    moves.append((d2_in, squares.at[1], d2_out))
+    loads = [pltpu.make_async_copy(src, mid, sem_in.at[i]) for i, (src, mid, _) in enumerate(moves)]
+    stores = [pltpu.make_async_copy(mid, dst, sem_out.at[i]) for i, (_, mid, dst) in enumerate(moves)]
+    for load in loads:
+        load.start()
+    for load, store in zip(loads, stores):
+        load.wait()
+        store.start()
+    for store in stores:
+        store.wait()
 
 
 def local(grad_trailing, panel_one, panel_two, grad_one, grad_two, inv_one, inv_two):
     any_space = pl.BlockSpec(memory_space=pl.ANY)
     vmem = pl.BlockSpec(memory_space=pltpu.VMEM)
     panel = jax.ShapeDtypeStruct(panel_one.shape, F32)
+    grouped = jax.ShapeDtypeStruct((8, 4, QUARTER, B), F32)
     square = jax.ShapeDtypeStruct((B, B), F32)
     dma = pltpu.SemaphoreType.DMA
     results = pl.pallas_call(
         kernel,
-        out_shape=(panel, panel, square, square),
+        out_shape=(grouped, grouped, square, square),
         in_specs=[any_space] * 5 + [vmem] * 2,
         out_specs=(any_space,) * 4,
         scratch_shapes=[
@@ -558,7 +622,8 @@
             pltpu.VMEM((BLOCKS, B, B), F32),
             pltpu.VMEM((BLOCKS, 2, HALF, B), F32),
             pltpu.VMEM((BLOCKS, HALF, B), F32),
-            pltpu.VMEM((2, 8, B, B), F32),
+            pltpu.VMEM((8 * BLOCKS, QUARTER, B), F32),
+            pltpu.VMEM((BLOCKS, B, B), F32),
             pltpu.VMEM((16, 32, B), F32),
             pltpu.VMEM((16, 16, B), F32),
             pltpu.VMEM((16, 32, B), F32),
@@ -574,14 +639,15 @@
             dma((BLOCKS,)),
             dma((BLOCKS,)),
             dma((BLOCKS, 2)),
-            dma((2, 8, 4)),
-            dma((BLOCKS, 8)),
+            dma((BLOCKS, 8, 4)),
+            dma((BLOCKS * 8,)),
             dma((4,)),
             dma((2, 16)),
             dma((2, 16)),
             dma((2, 16)),
-            dma((2, 16)),
-            dma((2, 2, 8)),
+            dma((2, 2)),
+            dma((2, 8)),
+            dma((2, 8)),
             dma,
             dma((16,)),
         ],
@@ -595,8 +661,14 @@
         out_shape=(panel, panel, square, square),
         in_specs=[any_space] * 4,
         out_specs=(any_space,) * 4,
-        scratch_shapes=[dma((4,))],
-    )(*results)
+        scratch_shapes=[
+            pltpu.VMEM((2, 8, B, B), F32),
+            pltpu.VMEM((2, B, B), F32),
+            dma((18,)),
+            dma((18,)),
+        ],
+        compiler_params=pltpu.CompilerParams(vmem_limit_bytes=16 * 2**20),
+    )(results[0].reshape(panel.shape), results[1].reshape(panel.shape), *results[2:])
 
 
 def solution(mesh):

time: 220 us -> 81.3 us (0.37)
  Pallas kernels: 220 us -> 75.4 us
  local copies, waits for them, and re-layouts: 0 us -> 5.07 us
    pallas_call x1, Pallas kernels: 144 us -> 2.8 us  [local(): pl.pallas_call(hand_over, out_shape=(panel, panel, square, square), in_sp...]
    unnamed x0 -> x8, local copies, waits for them, and re-layouts: none -> 5.07 us
    pallas_call x1, Pallas kernels: 75.5 us -> 72.6 us  [local(): pl.pallas_call(kernel, out_shape=(grouped, grouped, square, square), in_s...]
where the time goes in v2:
time: 81.3 us; the launch traced here: 81.1 us
  Pallas kernels  75.4 us (93%)
  local copies, waits for them, and re-layouts  5.07 us (6%)
    pallas_call x1, Pallas kernels, local(): pl.pallas_call(kernel, out_shape=(grouped, grouped, square, square), in_s...  72.6 us
    unnamed x8, local copies, waits for them, and re-layouts  5.07 us
    pallas_call x1, Pallas kernels, local(): pl.pallas_call(hand_over, out_shape=(panel, panel, square, square), in_sp...  2.8 us

profile of v2, /device:TPU:2, one launch (start us, length us, event | category | flops | bytes accessed | tf_op | source)
XLA Modules:
  0.0 81.1 jit_solution(17037356392925695566)
XLA Ops:
  0.6 72.6 %shard_map.102 = (f32[8,4,64,256]{3,2,1,0:T(8,128)}, f32[8,4,64,256]{3,2,1,0:T(8,128)}, f32[256,256]{1,0:T(8,128)}, f32[256,256]{1,0:T(8,128)}) custom-call(f32[8,1,256,4,1,256]{5,4,3,2,1,0:T(1,128)} %g_hbm.1, f32[8,1,256,256]{3,2,1,0:T(8,128)} %l1_hbm.1, f32[8,1,256,256]{3,2,1,0:T(8,128)} %l2_hbm.1, f32[8,1,256,256]{3,2,1,0:T(8,128)} %h1_hbm.1, ...), custom_call_target="tpu_custom_call" | custom-call | flops 7000000000 | bytes 22000000 | tf_op jit(solution)/shard_map/pallas_call | solution.py:604
  73.2 0.0 copy-start
  73.2 1.6 %copy-done = f32[8,4,64,256]{3,2,1,0:T(8,128)S(1)} copy-done((f32[8,4,64,256]{3,2,1,0:T(8,128)S(1)}, f32[8,4,64,256]{3,2,1,0:T(8,128)}, u32[]{:S(2)}) %copy-start) | copy-done | bytes 2097176
  74.8 0.0 copy-start.1
  74.8 1.6 %copy-done.1 = f32[8,4,64,256]{3,2,1,0:T(8,128)S(1)} copy-done((f32[8,4,64,256]{3,2,1,0:T(8,128)S(1)}, f32[8,4,64,256]{3,2,1,0:T(8,128)}, u32[]{:S(2)}) %copy-start.1) | copy-done | bytes 2097176
  76.4 0.0 copy-start.2
  76.4 0.9 %copy-done.2 = f32[256,256]{1,0:T(8,128)S(1)} copy-done((f32[256,256]{1,0:T(8,128)S(1)}, f32[256,256]{1,0:T(8,128)}, u32[]{:S(2)}) %copy-start.2) | copy-done | bytes 262168
  77.3 0.0 copy-start.3
  77.3 0.9 %copy-done.3 = f32[256,256]{1,0:T(8,128)S(1)} copy-done((f32[256,256]{1,0:T(8,128)S(1)}, f32[256,256]{1,0:T(8,128)}, u32[]{:S(2)}) %copy-start.3) | copy-done | bytes 262168
  78.3 2.8 %shard_map.103 = (f32[8,1,256,256]{3,2,1,0:T(8,128)}, f32[8,1,256,256]{3,2,1,0:T(8,128)}, f32[256,256]{1,0:T(8,128)}, f32[256,256]{1,0:T(8,128)}) custom-call(f32[8,1,256,256]{3,2,1,0:T(8,128)S(1)} %bitcast.2, f32[8,1,256,256]{3,2,1,0:T(8,128)S(1)} %bitcast.3, f32[256,256]{1,0:T(8,128)S(1)} %copy-done.2, f32[256,256]{1,0:T(8,128)S(1)} %copy-done.3), custom_call_target="tpu_custom_call" | custom-call | tf_op jit(solution)/shard_map/pallas_call | solution.py:659
Async XLA Ops:
  73.2 1.6 %copy-start = (f32[8,4,64,256]{3,2,1,0:T(8,128)S(1)}, f32[8,4,64,256]{3,2,1,0:T(8,128)}, u32[]{:S(2)}) copy-start(f32[8,4,64,256]{3,2,1,0:T(8,128)} %get-tuple-element.8) | copy-start | bytes 6291460
  74.8 1.6 %copy-start.1 = (f32[8,4,64,256]{3,2,1,0:T(8,128)S(1)}, f32[8,4,64,256]{3,2,1,0:T(8,128)}, u32[]{:S(2)}) copy-start(f32[8,4,64,256]{3,2,1,0:T(8,128)} %get-tuple-element.9) | copy-start | bytes 6291460
  76.4 0.9 %copy-start.2 = (f32[256,256]{1,0:T(8,128)S(1)}, f32[256,256]{1,0:T(8,128)}, u32[]{:S(2)}) copy-start(f32[256,256]{1,0:T(8,128)} %get-tuple-element.10.d1_in) | copy-start | bytes 786436
  77.3 0.9 %copy-start.3 = (f32[256,256]{1,0:T(8,128)S(1)}, f32[256,256]{1,0:T(8,128)}, u32[]{:S(2)}) copy-start(f32[256,256]{1,0:T(8,128)} %get-tuple-element.11.d2_in) | copy-start | bytes 786436

commit v3 on v2

--- a/solution.py
+++ b/solution.py
@@ -19,11 +19,10 @@
 DEPTH = (0, 3, 4, 3, 1, 2, 3, 2, 2, 3, 4, 3, 3, 4, 5, 4)
 DEEPEST = max(DEPTH)
 BLOCKS = 8
-HOP = 3
-START = 1 + 3 * HOP
+HOP = 2
+START = 2 + 3 * HOP
 TREE = 2
-FINISHED = (1, 3, 4, 6, 7, 7, 7, 8)
-SPREAD = (2, 7)
+SPREAD = (3, 7)
 OWN = (5, 10)
 COLUMN = (8, 13)
 LAST = BLOCKS - 1 + TREE * DEEPEST
@@ -111,8 +110,8 @@
             children = lookup(CHILDREN, 4 * u + v)
             depth = lookup(DEPTH, 4 * u + v)
             has = [(children // (1 << e)) % 2 == 1 for e in range(4)]
-            first = jnp.where(children > 0, TREE * depth, NEVER)
-            flows.append((turn_by, has, depth > 0, first, children > 0))
+            first = jnp.where(jnp.logical_and(children > 0, depth > 0), TREE * depth, NEVER)
+            flows.append((turn_by, has, first, children > 0))
     sides = (4 * y + (x + 1) % 4, 4 * ((y + 1) % 4) + x, 4 * y + (x + 3) % 4, 4 * ((y + 3) % 4) + x)
 
     barrier = pltpu.get_barrier_semaphore()
@@ -261,8 +260,7 @@
         col = (n + 1) % 4
         r = 2 * col + q // 8
         total = whole_sum(n)
-        load_h(0, col).wait()
-        resid = hbuf[0, col].T - 2.0 * total
+        resid = hbuf[0, col] - 2.0 * total
         at = turned_dot3(0, resid)
         obuf[pl.ds(8 * n + 4 * (q // 8), 4)] = at.T.reshape(4, QUARTER, B)
         atbuf[n] = at
@@ -279,8 +277,7 @@
         col = (n + 1) % 4
         r = 2 * col + q // 8
         total = whole_sum(n)
-        load_h(1, col).wait()
-        resid = hbuf[1, col].T - 2.0 * total - zbuf[col]
+        resid = hbuf[1, col] - 2.0 * total - zbuf[col]
         xbuf[n] = resid
 
         @pl.when(jnp.logical_and(is_root, n == 7))
@@ -370,7 +367,7 @@
 
     def store(n):
         for f in range(8):
-            @pl.when(jnp.logical_not(flows[f][4]))
+            @pl.when(jnp.logical_not(flows[f][3]))
             def _(f=f):
                 branch(n, f, 0).wait_recv()
 
@@ -386,15 +383,19 @@
             def _(r=r, tile=tile):
                 pltpu.make_async_copy(tile, a1_hbm.at[r], osem.at[1]).start()
 
+    def set_out(n):
+        for turn_by in range(4):
+            f = 4 * (q // 8) + turn_by
+            part = obuf.at[8 * n + f]
+            remote(part, part, tsend.at[n, f, 0], trecv.at[8 * n + f], p, sides[turn_by]).start()
+
     def forward(since, f):
-        _, has, below, first, _ = flows[f]
+        _, has, first, _ = flows[f]
         n = since - first
 
         @pl.when(jnp.logical_and(n >= 0, n < BLOCKS))
         def _():
-            @pl.when(below)
-            def _():
-                branch(n, f, 0).wait_recv()
+            branch(n, f, 0).wait_recv()
 
             for e in range(4):
                 @pl.when(has[e])
@@ -440,6 +441,13 @@
     def _():
         dacc2[...] = jnp.zeros_like(dacc2)
         dacc1[...] = jnp.zeros_like(dacc1)
+        for panel in range(2):
+            def turn_h(col, _, panel=panel):
+                load_h(panel, col).wait()
+                hbuf[panel, col] = hbuf[panel, col].T
+                return 0
+
+            lax.fori_loop(0, 4, turn_h, 0)
         keep_turned(0, w2_ref[...])
         keep_turned(1, w1_ref[...])
         corner_here.wait()
@@ -448,40 +456,29 @@
     def finish_step(since, _):
         chain_turn(START + since)
 
-        def finish(n, _):
-            @pl.when(n < 4)
+        @pl.when(is_dest)
+        def _():
+            @pl.when(since < 4)
             def _():
-                finish_two(n)
-
-            @pl.when(n >= 4)
+                finish_two(since)
+
+            @pl.when(since >= 4)
             def _():
-                finish_one(n)
-
-            return 0
-
-        def sums(n, _):
-            @pl.when(n < 4)
+                finish_one(since)
+
+            set_out(since)
+
+        pass_all(since)
+
+        @pl.when(is_dest)
+        def _():
+            @pl.when(since < 4)
             def _():
-                sums_two(n)
-
-            @pl.when(n >= 4)
+                sums_two(since)
+
+            @pl.when(since >= 4)
             def _():
-                sums_one(n)
-
-            return 0
-
-        before = lookup((0,) + FINISHED, since)
-        after = lookup(FINISHED, since)
-
-        @pl.when(is_dest)
-        def _():
-            lax.fori_loop(before, after, finish, 0)
-
-        pass_all(since)
-
-        @pl.when(is_dest)
-        def _():
-            lax.fori_loop(before, after, sums, 0)
+                sums_one(since)
 
             for rnd in range(2):
                 @pl.when(since == SPREAD[rnd])
@@ -494,7 +491,7 @@
 
         return 0
 
-    lax.fori_loop(0, len(FINISHED), finish_step, 0)
+    lax.fori_loop(0, BLOCKS, finish_step, 0)
 
     def last_step(since, _):
         pass_all(since)
@@ -512,7 +509,7 @@
 
         return 0
 
-    lax.fori_loop(len(FINISHED), LAST + 1, last_step, 0)
+    lax.fori_loop(BLOCKS, LAST + 1, last_step, 0)
 
     for rnd, out in ((0, d2_hbm), (1, d1_hbm)):
         def late(i, _, rnd=rnd):

time: 81.3 us -> 80.3 us (0.988)
  Pallas kernels: 75.4 us -> 74.3 us
    pallas_call x1, Pallas kernels: 72.6 us -> 71.5 us  [local(): pl.pallas_call(kernel, out_shape=(grouped, grouped, square, square), in_s...]
where the time goes in v3:
time: 80.3 us; the launch traced here: 80 us
  Pallas kernels  74.3 us (93%)
  local copies, waits for them, and re-layouts  5.07 us (6%)
    pallas_call x1, Pallas kernels, local(): pl.pallas_call(kernel, out_shape=(grouped, grouped, square, square), in_s...  71.5 us
    unnamed x8, local copies, waits for them, and re-layouts  5.07 us
    pallas_call x1, Pallas kernels, local(): pl.pallas_call(hand_over, out_shape=(panel, panel, square, square), in_sp...  2.8 us

profile of v3, /device:TPU:2, one launch (start us, length us, event | category | flops | bytes accessed | tf_op | source)
XLA Modules:
  0.0 80.0 jit_solution(15505570151504475539)
XLA Ops:
  0.6 71.5 %shard_map.102 = (f32[8,4,64,256]{3,2,1,0:T(8,128)}, f32[8,4,64,256]{3,2,1,0:T(8,128)}, f32[256,256]{1,0:T(8,128)}, f32[256,256]{1,0:T(8,128)}) custom-call(f32[8,1,256,4,1,256]{5,4,3,2,1,0:T(1,128)} %g_hbm.1, f32[8,1,256,256]{3,2,1,0:T(8,128)} %l1_hbm.1, f32[8,1,256,256]{3,2,1,0:T(8,128)} %l2_hbm.1, f32[8,1,256,256]{3,2,1,0:T(8,128)} %h1_hbm.1, ...), custom_call_target="tpu_custom_call" | custom-call | flops 7000000000 | bytes 22000000 | tf_op jit(solution)/shard_map/pallas_call | solution.py:601
  72.1 0.0 copy-start
  72.1 1.6 %copy-done = f32[8,4,64,256]{3,2,1,0:T(8,128)S(1)} copy-done((f32[8,4,64,256]{3,2,1,0:T(8,128)S(1)}, f32[8,4,64,256]{3,2,1,0:T(8,128)}, u32[]{:S(2)}) %copy-start) | copy-done | bytes 2097176
  73.7 0.0 copy-start.1
  73.7 1.6 %copy-done.1 = f32[8,4,64,256]{3,2,1,0:T(8,128)S(1)} copy-done((f32[8,4,64,256]{3,2,1,0:T(8,128)S(1)}, f32[8,4,64,256]{3,2,1,0:T(8,128)}, u32[]{:S(2)}) %copy-start.1) | copy-done | bytes 2097176
  75.3 0.0 copy-start.2
  75.3 0.9 %copy-done.2 = f32[256,256]{1,0:T(8,128)S(1)} copy-done((f32[256,256]{1,0:T(8,128)S(1)}, f32[256,256]{1,0:T(8,128)}, u32[]{:S(2)}) %copy-start.2) | copy-done | bytes 262168
  76.3 0.0 copy-start.3
  76.3 0.9 %copy-done.3 = f32[256,256]{1,0:T(8,128)S(1)} copy-done((f32[256,256]{1,0:T(8,128)S(1)}, f32[256,256]{1,0:T(8,128)}, u32[]{:S(2)}) %copy-start.3) | copy-done | bytes 262168
  77.2 2.8 %shard_map.103 = (f32[8,1,256,256]{3,2,1,0:T(8,128)}, f32[8,1,256,256]{3,2,1,0:T(8,128)}, f32[256,256]{1,0:T(8,128)}, f32[256,256]{1,0:T(8,128)}) custom-call(f32[8,1,256,256]{3,2,1,0:T(8,128)S(1)} %bitcast.2, f32[8,1,256,256]{3,2,1,0:T(8,128)S(1)} %bitcast.3, f32[256,256]{1,0:T(8,128)S(1)} %copy-done.2, f32[256,256]{1,0:T(8,128)S(1)} %copy-done.3), custom_call_target="tpu_custom_call" | custom-call | tf_op jit(solution)/shard_map/pallas_call | solution.py:656
Async XLA Ops:
  72.1 1.6 %copy-start = (f32[8,4,64,256]{3,2,1,0:T(8,128)S(1)}, f32[8,4,64,256]{3,2,1,0:T(8,128)}, u32[]{:S(2)}) copy-start(f32[8,4,64,256]{3,2,1,0:T(8,128)} %get-tuple-element.8) | copy-start | bytes 6291460
  73.7 1.6 %copy-start.1 = (f32[8,4,64,256]{3,2,1,0:T(8,128)S(1)}, f32[8,4,64,256]{3,2,1,0:T(8,128)}, u32[]{:S(2)}) copy-start(f32[8,4,64,256]{3,2,1,0:T(8,128)} %get-tuple-element.9) | copy-start | bytes 6291460
  75.3 0.9 %copy-start.2 = (f32[256,256]{1,0:T(8,128)S(1)}, f32[256,256]{1,0:T(8,128)}, u32[]{:S(2)}) copy-start(f32[256,256]{1,0:T(8,128)} %get-tuple-element.10.d1_in) | copy-start | bytes 786436
  76.3 0.9 %copy-start.3 = (f32[256,256]{1,0:T(8,128)S(1)}, f32[256,256]{1,0:T(8,128)}, u32[]{:S(2)}) copy-start(f32[256,256]{1,0:T(8,128)} %get-tuple-element.11.d2_in) | copy-start | bytes 786436

commit v4 on v3

--- a/solution.py
+++ b/solution.py
@@ -90,9 +90,9 @@
         return pltpu.make_async_copy(src.at[2 * col + q // 8, 0], hbuf.at[panel, col], hsem.at[panel, col])
 
     load_l(0).start()
-    load_l(1).start()
     for i in range(4):
         load_g((i + 1) % 4).start()
+    load_l(1).start()
 
     @pl.when(is_dest)
     def _():

time: 80.3 us -> 80.3 us (level)
  no operation moved by 1% of the time
where the time goes in v4:
time: 80.3 us; the launch traced here: 80 us
  Pallas kernels  74.3 us (93%)
  local copies, waits for them, and re-layouts  5.07 us (6%)
    pallas_call x1, Pallas kernels, local(): pl.pallas_call(kernel, out_shape=(grouped, grouped, square, square), in_s...  71.5 us
    unnamed x8, local copies, waits for them, and re-layouts  5.07 us
    pallas_call x1, Pallas kernels, local(): pl.pallas_call(hand_over, out_shape=(panel, panel, square, square), in_sp...  2.8 us

profile of v4, /device:TPU:2, one launch (start us, length us, event | category | flops | bytes accessed | tf_op | source)
XLA Modules:
  0.0 80.0 jit_solution(2246588004631139912)
XLA Ops:
  0.6 71.5 %shard_map.102 = (f32[8,4,64,256]{3,2,1,0:T(8,128)}, f32[8,4,64,256]{3,2,1,0:T(8,128)}, f32[256,256]{1,0:T(8,128)}, f32[256,256]{1,0:T(8,128)}) custom-call(f32[8,1,256,4,1,256]{5,4,3,2,1,0:T(1,128)} %g_hbm.1, f32[8,1,256,256]{3,2,1,0:T(8,128)} %l1_hbm.1, f32[8,1,256,256]{3,2,1,0:T(8,128)} %l2_hbm.1, f32[8,1,256,256]{3,2,1,0:T(8,128)} %h1_hbm.1, ...), custom_call_target="tpu_custom_call" | custom-call | flops 7000000000 | bytes 22000000 | tf_op jit(solution)/shard_map/pallas_call | solution.py:601
  72.1 0.0 copy-start
  72.1 1.6 %copy-done = f32[8,4,64,256]{3,2,1,0:T(8,128)S(1)} copy-done((f32[8,4,64,256]{3,2,1,0:T(8,128)S(1)}, f32[8,4,64,256]{3,2,1,0:T(8,128)}, u32[]{:S(2)}) %copy-start) | copy-done | bytes 2097176
  73.7 0.0 copy-start.1
  73.7 1.6 %copy-done.1 = f32[8,4,64,256]{3,2,1,0:T(8,128)S(1)} copy-done((f32[8,4,64,256]{3,2,1,0:T(8,128)S(1)}, f32[8,4,64,256]{3,2,1,0:T(8,128)}, u32[]{:S(2)}) %copy-start.1) | copy-done | bytes 2097176
  75.3 0.0 copy-start.2
  75.3 0.9 %copy-done.2 = f32[256,256]{1,0:T(8,128)S(1)} copy-done((f32[256,256]{1,0:T(8,128)S(1)}, f32[256,256]{1,0:T(8,128)}, u32[]{:S(2)}) %copy-start.2) | copy-done | bytes 262168
  76.3 0.0 copy-start.3
  76.3 0.9 %copy-done.3 = f32[256,256]{1,0:T(8,128)S(1)} copy-done((f32[256,256]{1,0:T(8,128)S(1)}, f32[256,256]{1,0:T(8,128)}, u32[]{:S(2)}) %copy-start.3) | copy-done | bytes 262168
  77.2 2.8 %shard_map.103 = (f32[8,1,256,256]{3,2,1,0:T(8,128)}, f32[8,1,256,256]{3,2,1,0:T(8,128)}, f32[256,256]{1,0:T(8,128)}, f32[256,256]{1,0:T(8,128)}) custom-call(f32[8,1,256,256]{3,2,1,0:T(8,128)S(1)} %bitcast.2, f32[8,1,256,256]{3,2,1,0:T(8,128)S(1)} %bitcast.3, f32[256,256]{1,0:T(8,128)S(1)} %copy-done.2, f32[256,256]{1,0:T(8,128)S(1)} %copy-done.3), custom_call_target="tpu_custom_call" | custom-call | tf_op jit(solution)/shard_map/pallas_call | solution.py:656
Async XLA Ops:
  72.1 1.6 %copy-start = (f32[8,4,64,256]{3,2,1,0:T(8,128)S(1)}, f32[8,4,64,256]{3,2,1,0:T(8,128)}, u32[]{:S(2)}) copy-start(f32[8,4,64,256]{3,2,1,0:T(8,128)} %get-tuple-element.8) | copy-start | bytes 6291460
  73.7 1.6 %copy-start.1 = (f32[8,4,64,256]{3,2,1,0:T(8,128)S(1)}, f32[8,4,64,256]{3,2,1,0:T(8,128)}, u32[]{:S(2)}) copy-start(f32[8,4,64,256]{3,2,1,0:T(8,128)} %get-tuple-element.9) | copy-start | bytes 6291460
  75.3 0.9 %copy-start.2 = (f32[256,256]{1,0:T(8,128)S(1)}, f32[256,256]{1,0:T(8,128)}, u32[]{:S(2)}) copy-start(f32[256,256]{1,0:T(8,128)} %get-tuple-element.10.d1_in) | copy-start | bytes 786436
  76.3 0.9 %copy-start.3 = (f32[256,256]{1,0:T(8,128)S(1)}, f32[256,256]{1,0:T(8,128)}, u32[]{:S(2)}) copy-start(f32[256,256]{1,0:T(8,128)} %get-tuple-element.11.d2_in) | copy-start | bytes 786436
